TPU v7x, 32 devices: a whole 2x2x4 slice. The times are simulated.
32 devices in a mesh: row: 4 (over x, core), col: 8 (over z, y).
Axes of the slice: x: 2, y: 2, z: 4, core: 2. Of those that a mesh axis runs over, the one named last changes fastest.
Arguments:
- src_points: bfloat16 [1024, 256], P(('row', 'col')), may hold values from -16 to 16, as said below
- tgt_points: bfloat16 [1024, 256], P(('col', 'row')), may hold values from -16 to 16, as said below
- log_src: float32 [1024], P('row'), may hold values from -144 to 4, as said below
- log_tgt: float32 [1024], P('col'), may hold values from -4 to 4
- tgt_potential: float32 [1024], P('col'), may hold values from -7680 to 7680
Outputs:
- src_potential: float32 [1024], P('row')
- new_tgt_potential: float32 [1024], P('col')
- src_map: bfloat16 [1024, 256], P(('row', 'col'))
- tgt_map: bfloat16 [1024, 256], P(('col', 'row'))
Inputs may be any that keep to these rules, and one draw needn't show every extreme that they name: `src_points`: coordinates of source codes. `tgt_points`: coordinates of target codes. `log_src`: unnormalised log-weights of the source points.
All inputs are finite; a program needn't handle non-finite values.
Results may differ from a plain program's by a relative error of at most 0.0033.
The roundings to bfloat16 on the way count: a program that leaves them out, or rounds other values in their place, can miss the bound.
Values may be sent and summed in bfloat16 or wider, within the bound.
A program may use at most 64 MiB of HBM per device.

v0:
```python
import math

import jax
import jax.numpy as jnp
from jax import lax
from jax.sharding import PartitionSpec as P

D = 256


def cost_rows(src_block, targets, tgt_sq):
    src_sq = jnp.sum(jnp.square(src_block.astype(jnp.float32)), axis=1)
    inner = jnp.dot(src_block, targets.T, preferred_element_type=jnp.float32)
    return (src_sq[:, None] + tgt_sq[None, :] - 2.0 * inner).astype(jnp.bfloat16)


def widen(tile):
    return lax.optimization_barrier(tile).astype(jnp.float32)


def body(src_points, tgt_points, log_src, log_tgt, tgt_potential):
    epsilon = 0.1 * D
    sources = lax.all_gather(src_points, "col", axis=0, tiled=True)
    targets = lax.all_gather(tgt_points, "row", axis=0, tiled=True)
    src_rows, features = sources.shape
    tgt_rows = targets.shape[0]
    own_rows = src_points.shape[0]
    block_rows = math.gcd(src_rows, 512)
    blocks = src_rows // block_rows
    tgt_sq = jnp.sum(jnp.square(targets.astype(jnp.float32)), axis=1)
    src_blocks = sources.reshape(blocks, block_rows, features)

    def load(src_block):
        return widen(cost_rows(src_block, targets, tgt_sq))

    tiles = (src_blocks, src_blocks)

    def row_scores(element, potential):
        costs = load(element[0])
        return log_tgt[None, :] + (potential[None, :] - costs) / epsilon

    def row_lse(potential):

        def top_rows(element):
            return jnp.max(row_scores(element, potential), axis=1)

        highest = lax.pmax(lax.map(top_rows, tiles).reshape(src_rows), "col")

        def mass_rows(element):
            scores = row_scores(element[0], potential)
            return jnp.sum(jnp.exp(scores - element[1][:, None]), axis=1)

        partial_mass = lax.map(mass_rows, (tiles, highest.reshape(blocks, block_rows)))
        totals = lax.psum(partial_mass.reshape(src_rows), "col")
        return highest + jnp.log(totals)

    src_potential = -epsilon * row_lse(tgt_potential)
    log_blocks = log_src.reshape(blocks, block_rows)
    pot_blocks = src_potential.reshape(blocks, block_rows)
    column_feed = (tiles, log_blocks, pot_blocks)

    def column_scores(element):
        pieces, log_block, pot_block = element
        costs = load(pieces[0])
        return log_block[:, None] + (pot_block[:, None] - costs) / epsilon

    def fold_top(running, element):
        return (jnp.maximum(running, jnp.max(column_scores(element), axis=0)), None)

    highest, _ = lax.scan(fold_top, jnp.full((tgt_rows,), -jnp.inf, jnp.float32), column_feed)
    highest = lax.pmax(highest, "row")

    def fold_mass(running, element):
        return (running + jnp.sum(jnp.exp(column_scores(element) - highest[None, :]), axis=0), None)

    totals, _ = lax.scan(fold_mass, jnp.zeros((tgt_rows,), jnp.float32), column_feed)
    totals = lax.psum(totals, "row")
    new_tgt_potential = -epsilon * (highest + jnp.log(totals))
    map_lse = row_lse(new_tgt_potential)

    def map_fold(running, element):
        pieces, log_block, pot_block, lse_block = element
        costs = load(pieces[0])
        scores = log_tgt[None, :] + (new_tgt_potential[None, :] - costs) / epsilon
        forward = jnp.exp(scores - lse_block[:, None]).astype(jnp.bfloat16)
        src_part = jnp.dot(forward, targets, preferred_element_type=jnp.float32)
        backward = jnp.exp(
            log_block[:, None]
            + (pot_block[:, None] - costs) / epsilon
            + new_tgt_potential[None, :] / epsilon
        ).astype(jnp.bfloat16)
        return (
            running + jnp.dot(backward.T, pieces[0], preferred_element_type=jnp.float32),
            src_part,
        )

    map_feed = (tiles, log_blocks, pot_blocks, map_lse.reshape(blocks, block_rows))
    tgt_partial, src_parts = lax.scan(
        map_fold, jnp.zeros((tgt_rows, features), jnp.float32), map_feed
    )
    src_partial = src_parts.reshape(src_rows, features)
    src_whole = lax.psum(src_partial, "col")
    tgt_whole = lax.psum(tgt_partial, "row")
    src_map = lax.dynamic_slice_in_dim(src_whole, lax.axis_index("col") * own_rows, own_rows, 0)
    tgt_map = lax.dynamic_slice_in_dim(tgt_whole, lax.axis_index("row") * own_rows, own_rows, 0)
    return (
        src_potential,
        new_tgt_potential,
        src_map.astype(jnp.bfloat16),
        tgt_map.astype(jnp.bfloat16),
    )


def solution(mesh):
    in_specs = (P(("row", "col"), None), P(("col", "row"), None), P("row"), P("col"), P("col"))
    out_specs = (P("row"), P("col"), P(("row", "col"), None), P(("col", "row"), None))
    return jax.shard_map(body, mesh=mesh, in_specs=in_specs, out_specs=out_specs, check_vma=False)
```

profile of v0, /device:TPU:0, one launch (start us, length us, event | category | flops | bytes accessed | tf_op | source)
XLA Modules:
  0.0 181.1 jit_solution(12580646894400831670)
XLA Ops:
  0.6 0.0 copy-start.1
  0.6 0.7 copy-done.1
  1.3 6.1 %all_gather.7 = bf16[128,256]{1,0:T(8,128)(2,1)S(1)} all-gather(bf16[32,256]{1,0:T(8,128)(2,1)S(1)} %copy-done.1), channel_id=1, replica_groups=mesh['row'=4,'col'=8] {'row'}, dimensions={0}, use_global_device_ids=true | all-gather | bytes 81920 | tf_op jit(solution)/shard_map/all_gather | solution.py:24
  7.5 0.0 copy-start.2
  7.5 0.1 multiply_reduce_fusion.1
  7.6 0.6 copy-done.2
  8.2 31.4 %all_gather.6 = bf16[256,256]{1,0:T(8,128)(2,1)S(1)} all-gather(bf16[32,256]{1,0:T(8,128)(2,1)S(1)} %copy-done.2), channel_id=1, replica_groups=mesh['row'=4,'col'=8] {'col'}, dimensions={0}, use_global_device_ids=true | all-gather | bytes 147456 | tf_op jit(solution)/shard_map/all_gather | solution.py:23
  39.6 0.1 multiply_reduce_fusion
  39.7 0.0 copy-start.3
  39.7 0.0 copy-start.6
  39.7 0.2 fusion.1
  39.9 0.4 copy-done.3
  40.4 0.0 copy-done.6
  40.4 0.1 fusion.5
  40.5 21.3 %pmax.21 = f32[256]{0:T(256)S(1)} all-reduce(f32[256]{0:T(256)S(1)} %fusion.5), channel_id=1, replica_groups=mesh['row'=4,'col'=8] {'col'}, use_global_device_ids=true, to_apply=%region_3.0 | all-reduce | flops 256 | bytes 2048 | tf_op jit(solution)/shard_map/pmax | solution.py:47
  61.8 0.2 fusion.7
  62.0 17.1 %psum.35 = f32[256]{0:T(256)S(1)} all-reduce(f32[256]{0:T(256)S(1)} %fusion.7), channel_id=1, replica_groups=mesh['row'=4,'col'=8] {'col'}, use_global_device_ids=true, to_apply=%region_5.6 | all-reduce | flops 256 | bytes 2048 | tf_op jit(solution)/shard_map/psum | solution.py:54
  79.2 0.0 copy-start.4
  79.2 0.7 copy-done.4
  79.8 0.0 copy-start
  79.8 0.1 fusion.12
  80.0 5.7 %pmax.22 = f32[128]{0:T(128)S(1)} all-reduce(f32[128]{0:T(128)S(1)} %fusion.12), channel_id=1, replica_groups=mesh['row'=4,'col'=8] {'row'}, use_global_device_ids=true, to_apply=%region_7.8 | all-reduce | flops 128 | bytes 1024 | tf_op jit(solution)/shard_map/pmax | solution.py:71
  85.7 0.2 fusion.14
  85.8 6.6 %psum.36 = f32[128]{0:T(128)S(1)} all-reduce(f32[128]{0:T(128)S(1)} %fusion.14), channel_id=1, replica_groups=mesh['row'=4,'col'=8] {'row'}, use_global_device_ids=true, to_apply=%region_9.10 | all-reduce | flops 128 | bytes 1024 | tf_op jit(solution)/shard_map/psum | solution.py:77
  92.4 0.0 copy-start.5
  92.4 0.0 copy-done
  92.4 0.3 fusion.28
  92.8 12.3 %all-reduce.2 = bf16[128,256]{1,0:T(8,128)(2,1)S(1)} all-reduce(f32[128,256]{1,0:T(8,128)S(1)} %fusion.28), channel_id=1, replica_groups=mesh['row'=4,'col'=8] {'row'}, use_global_device_ids=true, to_apply=%region_15.16 | all-reduce | flops 32768 | bytes 196608 | tf_op jit(solution)/shard_map/psum | solution.py:103
  105.1 0.6 dynamic-slice_convert_fusion
  105.7 0.1 fusion.21
  105.8 19.1 %pmax.23 = f32[256]{0:T(256)S(1)} all-reduce(f32[256]{0:T(256)S(1)} %fusion.21), channel_id=1, replica_groups=mesh['row'=4,'col'=8] {'col'}, use_global_device_ids=true, to_apply=%region_11.12 | all-reduce | flops 256 | bytes 2048 | tf_op jit(solution)/shard_map/pmax | solution.py:47
  125.0 0.2 fusion.23
  125.1 17.2 %psum.37 = f32[256]{0:T(256)S(1)} all-reduce(f32[256]{0:T(256)S(1)} %fusion.23), channel_id=1, replica_groups=mesh['row'=4,'col'=8] {'col'}, use_global_device_ids=true, to_apply=%region_13.14 | all-reduce | flops 256 | bytes 2048 | tf_op jit(solution)/shard_map/psum | solution.py:54
  142.4 0.0 copy-done.5
  142.4 0.2 fusion.26
  142.6 37.8 %all-reduce.3 = bf16[256,256]{1,0:T(8,128)(2,1)S(1)} all-reduce(f32[256,256]{1,0:T(8,128)S(1)} %fusion.26), channel_id=1, replica_groups=mesh['row'=4,'col'=8] {'col'}, use_global_device_ids=true, to_apply=%region_14.15 | all-reduce | flops 65536 | bytes 393216 | tf_op jit(solution)/shard_map/psum | solution.py:102
  180.5 0.6 dynamic-slice_convert_fusion.1
  (3 shorter events, 0.0 us)
Async XLA Ops:
  0.6 0.7 copy-start.1
  7.5 0.7 copy-start.2
  39.7 0.7 copy-start.3
  39.7 0.7 copy-start.6
  79.2 0.7 copy-start.4
  79.8 12.6 %copy-start = (f32[256]{0:T(256)}, f32[256]{0:T(256)S(1)}, u32[]{:S(2)}) copy-start(f32[256]{0:T(256)S(1)} %add_multiply_fusion) | copy-start | bytes 3076
  92.4 50.0 %copy-start.5 = (f32[128]{0:T(128)}, f32[128]{0:T(128)S(1)}, u32[]{:S(2)}) copy-start(f32[128]{0:T(128)S(1)} %get-tuple-element.121) | copy-start | bytes 1540
where the time goes:
time: 182 us; the launch traced here: 181 us
  blocking collectives  175 us (96%)
  local copies, waits for them, and re-layouts  3.68 us (2%)
    pmax x2, blocking collectives, row_lse(): highest = lax.pmax(lax.map(top_rows, tiles).reshape(src_rows), 'col')  40.5 us
    psum x1, blocking collectives, body(): src_whole = lax.psum(src_partial, 'col')  37.8 us
    psum x2, blocking collectives, row_lse(): totals = lax.psum(partial_mass.reshape(src_rows), 'col')  34.4 us
    all_gather x1, blocking collectives, body(): sources = lax.all_gather(src_points, 'col', axis=0, tiled=True)  31.4 us
    psum x1, blocking collectives, body(): tgt_whole = lax.psum(tgt_partial, 'row')  12.3 us
    psum x1, blocking collectives, body(): totals = lax.psum(totals, 'row')  6.62 us
    all_gather x1, blocking collectives, body(): targets = lax.all_gather(tgt_points, 'row', axis=0, tiled=True)  6.15 us
    pmax x1, blocking collectives, body(): highest = lax.pmax(highest, 'row')  5.67 us

commit v1 on v0

v1 whole, which is shorter than its diff:
```python
import functools
import math

import jax
import jax.numpy as jnp
from jax import lax
from jax.experimental import pallas as pl
from jax.experimental.pallas import tpu as pltpu
from jax.sharding import PartitionSpec as P

MESH = pl.DeviceIdType.MESH
LOG2E = 1.0 / math.log(2.0)
LN2 = math.log(2.0)
NT_DIMS = (((1,), (1,)), ((), ()))
TN_DIMS = (((0,), (0,)), ((), ()))


def repeat(count, step):
    if count <= 8:
        for index in range(count):
            step(index)
    else:
        pl.loop(0, count)(step)


def block_of(index, size):
    start = index * size
    return pl.ds(start if isinstance(index, int) else pl.multiple_of(start, size), size)


def kernel(
    rows_n, cols_n,
    src_ref, tgt_ref, lsrc_ref, ltgt_ref, tpot_ref,
    spot_ref, npot_ref, smap_ref, tmap_ref,
    tgts, srcs, logs, cost, base, lse_cols, pair, pairs, part, parts,
    z_send, z_recv, y_send, y_recv, x_send, x_recv, c_send, c_recv,
    zs_send, zs_recv, ys_send, ys_recv, v_send, v_recv,
    m_send, m_recv, p_send, p_recv,
):
    row, col = lax.axis_index("row"), lax.axis_index("col")
    half_c, half_r = cols_n // 2, rows_n // 2
    zi, yi = col // 2, lax.rem(col, 2)
    xi, ci = row // 2, lax.rem(row, 2)
    own, width = tgt_ref.shape
    rows = cost.shape[0]
    targets = cost.shape[1]
    chunk = targets // half_c
    mine = targets // cols_n
    epsilon = 0.1 * width
    scale = LOG2E / epsilon

    def copy(src, dst, send, recv, to_row, to_col):
        return pltpu.make_async_remote_copy(
            src_ref=src, dst_ref=dst, send_sem=send, recv_sem=recv,
            device_id=(to_row, to_col), device_id_type=MESH,
        )

    barrier = pltpu.get_barrier_semaphore()
    for step in range(1, cols_n):
        pl.semaphore_signal(barrier, inc=1, device_id=(row, lax.rem(col + step, cols_n)), device_id_type=MESH)
    for step in range(1, rows_n):
        pl.semaphore_signal(barrier, inc=1, device_id=(lax.rem(row + step, rows_n), col), device_id_type=MESH)

    tgts[zi, yi, xi, ci] = tgt_ref[...]
    srcs[zi, yi] = src_ref[...]
    here = pl.ds(pl.multiple_of(col * mine, mine), mine)
    logs[0:1, here] = ltgt_ref[...]
    logs[1:2, here] = tpot_ref[...]
    pl.semaphore_wait(barrier, cols_n - 1 + rows_n - 1)

    other_y, other_c = 1 - yi, 1 - ci
    y_col = zi * 2 + other_y
    c_row = xi * 2 + other_c

    def z_copy(step):
        dst = lax.rem(zi + step, half_c)
        return copy(tgt_ref, tgts.at[zi, yi, xi, ci], z_send.at[step], z_recv.at[step], row, dst * 2 + yi)

    def zs_copy(step):
        dst = lax.rem(zi + step, half_c)
        return copy(src_ref, srcs.at[zi, yi], zs_send.at[step], zs_recv.at[step], row, dst * 2 + yi)

    def y_copy(step):
        which = lax.rem(zi - step + half_c, half_c)
        block = tgts.at[which, yi, xi, ci]
        return copy(block, block, y_send.at[step], y_recv.at[step], row, y_col)

    def ys_copy(step):
        which = lax.rem(zi - step + half_c, half_c)
        block = srcs.at[which, yi]
        return copy(block, block, ys_send.at[step], ys_recv.at[step], row, y_col)

    def x_copy(step, group):
        block = tgts.at[:, lax.rem(yi + group, 2), xi, ci]
        to_row = lax.rem(xi + step, half_r) * 2 + ci
        return copy(block, block, x_send.at[step, group], x_recv.at[step, group], to_row, col)

    def c_copy(step, group):
        which = lax.rem(xi - step + half_r, half_r)
        block = tgts.at[:, lax.rem(yi + group, 2), which, ci]
        return copy(block, block, c_send.at[step, group], c_recv.at[step, group], c_row, col)

    def v_copy(step):
        return copy(logs.at[:, here], logs.at[:, here], v_send.at[step], v_recv.at[step], row, lax.rem(col + step, cols_n))

    y_first = y_copy(0)
    y_first.start()
    for step in range(1, half_c):
        z_copy(step).start()
    ys_copy(0).start()
    for step in range(1, half_c):
        zs_copy(step).start()
    for step in range(1, cols_n):
        v_copy(step).start()

    for step in range(1, half_c):
        z_copy(step).wait_recv()
        y_copy(step).start()
    for step in range(1, half_r):
        x_copy(step, 0).start()
    c_copy(0, 0).start()
    for step in range(1, half_c):
        zs_copy(step).wait_recv()
        ys_copy(step).start()
    for step in range(half_c):
        y_copy(step).wait_recv()
    for step in range(1, half_r):
        x_copy(step, 1).start()
    c_copy(0, 1).start()
    for group in range(2):
        for step in range(1, half_r):
            x_copy(step, group).wait_recv()
            c_copy(step, group).start()
    for step in range(half_c):
        ys_copy(step).wait_recv()
    for step in range(1, cols_n):
        v_copy(step).wait_recv()
    for group in range(2):
        for step in range(half_r):
            c_copy(step, group).wait_recv()

    tall = math.gcd(rows, 256)
    blocks = tall // own
    flat = srcs.reshape(half_c * 2, own, width)

    def make_cost(index):
        span = block_of(index, chunk)
        tile = tgts[index].reshape(chunk, width)
        wide = tile.astype(jnp.float32)
        square = wide * wide
        high = square.astype(jnp.bfloat16)
        low = (square - high.astype(jnp.float32)).astype(jnp.bfloat16)
        ones = jnp.ones((16, width), jnp.bfloat16)
        dot = functools.partial(lax.dot_general, dimension_numbers=NT_DIMS, preferred_element_type=jnp.float32)
        tgt_sq = (dot(ones, high) + dot(ones, low))[0:1, :]

        def strip(part_index):
            src = flat[block_of(part_index, blocks)].reshape(tall, width)
            wide_src = src.astype(jnp.float32)
            src_sq = jnp.sum(wide_src * wide_src, axis=1, keepdims=True)
            value = (src_sq + tgt_sq) - 2.0 * dot(src, tile)
            cost[block_of(part_index, tall), span] = value.astype(jnp.bfloat16)

        repeat(rows // tall, strip)

    repeat(half_c, make_cost)

    forward_base = (logs[0:1, :] + logs[1:2, :] * (1.0 / epsilon)) * LOG2E

    def lse_rows(costs, offset):
        scores = offset - costs.astype(jnp.float32) * scale
        top = jnp.max(scores, axis=1, keepdims=True)
        mass = jnp.sum(jnp.exp2(scores - top), axis=1, keepdims=True)
        return top + jnp.log(mass) * LOG2E

    def first_pass(index):
        span = block_of(index, own)
        base[span, :] = jnp.broadcast_to(lse_rows(cost[span, :], forward_base), (own, base.shape[1]))

    repeat(rows // own, first_pass)
    spot_ref[...] = jnp.transpose(base[...])[0:1, :] * (-epsilon * LN2)
    source_logs = jnp.transpose(jnp.broadcast_to(lsrc_ref[...], (base.shape[1], rows)))
    base[...] = source_logs * LOG2E - base[...]

    def column_pass(index):
        span = block_of(index, chunk)
        scores = base[:, 0:1] - cost[:, span].astype(jnp.float32) * scale
        top = jnp.max(scores, axis=0, keepdims=True)
        pair[0:1, span] = top
        pair[1:2, span] = jnp.sum(jnp.exp2(scores - top), axis=0, keepdims=True)

    repeat(half_c, column_pass)

    def m_copy(step):
        return copy(pair, pairs.at[step - 1], m_send.at[step], m_recv.at[step], lax.rem(row + step, rows_n), col)

    for step in range(1, rows_n):
        m_copy(step).start()
    for step in range(1, rows_n):
        m_copy(step).wait_recv()
    tops = [pair[0:1, :]] + [pairs[step, 0:1, :] for step in range(rows_n - 1)]
    masses = [pair[1:2, :]] + [pairs[step, 1:2, :] for step in range(rows_n - 1)]
    highest = functools.reduce(jnp.maximum, tops)
    total = sum(mass * jnp.exp2(top - highest) for top, mass in zip(tops, masses))
    lse_cols[...] = highest + jnp.log(total) * LOG2E
    npot_ref[...] = lse_cols[0:1, here] * (-epsilon * LN2)

    backward = jnp.exp2(base[:, 0:1] - cost[:, here].astype(jnp.float32) * scale - lse_cols[0:1, here])
    sources = srcs[...].reshape(rows, width)
    partial = lax.dot_general(backward.astype(jnp.bfloat16), sources, TN_DIMS, preferred_element_type=jnp.float32)
    part[...] = partial.reshape(rows_n, own, width)

    def p_copy(step):
        to_row = lax.rem(row + step, rows_n)
        return copy(part.at[to_row], parts.at[step - 1], p_send.at[step], p_recv.at[step], to_row, col)

    for step in range(1, rows_n):
        p_copy(step).start()

    my_rows = pl.ds(pl.multiple_of(col * own, own), own)
    offset = logs[0:1, :] * LOG2E - lse_cols[...]
    map_lse = lse_rows(cost[my_rows, :], offset)
    smap = jnp.zeros((own, width), jnp.float32)

    def forward_part(index, running):
        span = block_of(index, chunk)
        move = logs[0:1, span] * LOG2E - lse_cols[0:1, span]
        weight = jnp.exp2((move - cost[my_rows, span].astype(jnp.float32) * scale) - map_lse)
        tile = tgts[index].reshape(chunk, width)
        return running + jnp.dot(weight.astype(jnp.bfloat16), tile, preferred_element_type=jnp.float32)

    if half_c <= 8:
        for index in range(half_c):
            smap = forward_part(index, smap)
    else:
        smap = lax.fori_loop(0, half_c, forward_part, smap)
    smap_ref[...] = smap.astype(jnp.bfloat16)

    for step in range(1, rows_n):
        p_copy(step).wait_recv()
    whole = part[row]
    for step in range(rows_n - 1):
        whole = whole + parts[step]
    tmap_ref[...] = whole.astype(jnp.bfloat16)

    for step in range(1, half_c):
        z_copy(step).wait_send()
        zs_copy(step).wait_send()
    for step in range(half_c):
        y_copy(step).wait_send()
        ys_copy(step).wait_send()
    for group in range(2):
        for step in range(half_r):
            if step:
                x_copy(step, group).wait_send()
            c_copy(step, group).wait_send()
    for step in range(1, cols_n):
        v_copy(step).wait_send()
    for step in range(1, rows_n):
        m_copy(step).wait_send()
        p_copy(step).wait_send()


def solution(mesh):
    rows_n, cols_n = mesh.shape["row"], mesh.shape["col"]
    half_c, half_r = cols_n // 2, rows_n // 2

    def body(src_points, tgt_points, log_src, log_tgt, tgt_potential):
        own, width = src_points.shape
        rows, mine = log_src.shape[0], log_tgt.shape[0]
        targets = mine * cols_n
        f32, bf16 = jnp.float32, jnp.bfloat16
        dma = pltpu.SemaphoreType.DMA
        vmem = pl.BlockSpec(memory_space=pltpu.VMEM)
        spot, npot, smap, tmap = pl.pallas_call(
            functools.partial(kernel, rows_n, cols_n),
            out_shape=(
                jax.ShapeDtypeStruct((1, rows), f32),
                jax.ShapeDtypeStruct((1, mine), f32),
                jax.ShapeDtypeStruct((own, width), bf16),
                jax.ShapeDtypeStruct((own, width), bf16),
            ),
            in_specs=[vmem] * 5,
            out_specs=(vmem,) * 4,
            scratch_shapes=[
                pltpu.VMEM((half_c, 2, half_r, 2, own, width), bf16),
                pltpu.VMEM((half_c, 2, own, width), bf16),
                pltpu.VMEM((2, targets), f32),
                pltpu.VMEM((rows, targets), bf16),
                pltpu.VMEM((rows, 128), f32),
                pltpu.VMEM((1, targets), f32),
                pltpu.VMEM((2, targets), f32),
                pltpu.VMEM((rows_n - 1, 2, targets), f32),
                pltpu.VMEM((rows_n, own, width), f32),
                pltpu.VMEM((rows_n - 1, own, width), f32),
                dma((half_c,)), dma((half_c,)),
                dma((half_c,)), dma((half_c,)),
                dma((half_r, 2)), dma((half_r, 2)),
                dma((half_r, 2)), dma((half_r, 2)),
                dma((half_c,)), dma((half_c,)),
                dma((half_c,)), dma((half_c,)),
                dma((cols_n,)), dma((cols_n,)),
                dma((rows_n,)), dma((rows_n,)),
                dma((rows_n,)), dma((rows_n,)),
            ],
            compiler_params=pltpu.CompilerParams(
                collective_id=0, has_side_effects=True, vmem_limit_bytes=56 * 1024 * 1024
            ),
        )(src_points, tgt_points, log_src[None, :], log_tgt[None, :], tgt_potential[None, :])
        return spot[0], npot[0], smap, tmap

    in_specs = (P(("row", "col"), None), P(("col", "row"), None), P("row"), P("col"), P("col"))
    out_specs = (P("row"), P("col"), P(("row", "col"), None), P(("col", "row"), None))
    return jax.shard_map(body, mesh=mesh, in_specs=in_specs, out_specs=out_specs, check_vma=False)
```

time: 182 us -> 29.9 us (0.16)
  blocking collectives: 175 us -> 0 us
  Pallas kernels: 0 us -> 25.2 us
    psum x5 -> x0, blocking collectives: 91.1 us -> none  [the longest x1 37.8 us: body(): src_whole = lax.psum(src_partial, 'col')]
    pmax x3 -> x0, blocking collectives: 46.1 us -> none  [the longest x2 40.5 us: row_lse(): highest = lax.pmax(lax.map(top_rows, tiles).reshape(src_rows), 'col')]
    all_gather x2 -> x0, blocking collectives: 37.5 us -> none  [the longest x1 31.4 us: body(): sources = lax.all_gather(src_points, 'col', axis=0, tiled=True)]
    pallas_call x0 -> x1, Pallas kernels: none -> 25.2 us  [body(): pl.pallas_call(functools.partial(kernel, rows_n, cols_n), out_shape=(jax....]
    unnamed x14 -> x10, local copies, waits for them, and re-layouts: 2.45 us -> 3.79 us
where the time goes in v1:
time: 29.9 us; the launch traced here: 29.6 us
  Pallas kernels  25.2 us (84%)
  local copies, waits for them, and re-layouts  3.79 us (13%)
  between operations  0.65 us (2%)
    pallas_call x1, Pallas kernels, body(): pl.pallas_call(functools.partial(kernel, rows_n, cols_n), out_shape=(jax....  25.2 us
    unnamed x10, local copies, waits for them, and re-layouts  3.79 us

profile of v1, /device:TPU:0, one launch (start us, length us, event | category | flops | bytes accessed | tf_op | source)
XLA Modules:
  0.0 29.6 jit_solution(14768362932729505804)
XLA Ops:
  0.6 25.2 %shard_map.84 = (f32[1,256]{1,0:T(1,128)}, f32[1,128]{1,0:T(1,128)}, bf16[32,256]{1,0:T(8,128)(2,1)}, bf16[32,256]{1,0:T(8,128)(2,1)}) custom-call(bf16[32,256]{1,0:T(8,128)(2,1)} %src_ref.1, bf16[32,256]{1,0:T(8,128)(2,1)} %tgt_ref.1, f32[1,256]{1,0:T(1,128)} %bitcast.5, f32[1,128]{1,0:T(1,128)} %bitcast.7, f32[1,128]{1,0:T(1,128)} %bitcast.8), custom_call_target="tpu_custom_call" | custom-call | tf_op jit(solution)/shard_map/pallas_call | solution.py:275
  25.8 0.0 copy-start.1
  25.8 0.7 %copy-done.1 = f32[1,256]{1,0:T(1,128)S(1)} copy-done((f32[1,256]{1,0:T(1,128)S(1)}, f32[1,256]{1,0:T(1,128)}, u32[]{:S(2)}) %copy-start.1) | copy-done | bytes 1048
  26.5 0.0 copy-start.2
  26.5 0.6 %copy.13 = f32[256]{0:T(256)} copy(f32[256]{0:T(256)S(1)} %bitcast.6) | data formatting | bytes 2048
  27.1 0.1 copy-done.2
  27.2 0.5 %copy.14 = f32[128]{0:T(128)} copy(f32[128]{0:T(128)S(1)} %bitcast.9) | data formatting | bytes 1024
  27.7 0.0 copy-start
  27.7 1.3 %copy.15 = bf16[32,256]{1,0:T(8,128)(2,1)} copy(bf16[32,256]{1,0:T(8,128)(2,1)} %get-tuple-element.18) | data formatting | bytes 32768
  29.0 0.0 copy-done
  29.0 0.6 %copy.16 = bf16[32,256]{1,0:T(8,128)(2,1)} copy(bf16[32,256]{1,0:T(8,128)(2,1)S(1)} %copy-done) | data formatting | bytes 32768
Async XLA Ops:
  25.8 0.7 %copy-start.1 = (f32[1,256]{1,0:T(1,128)S(1)}, f32[1,256]{1,0:T(1,128)}, u32[]{:S(2)}) copy-start(f32[1,256]{1,0:T(1,128)} %get-tuple-element.8) | copy-start | bytes 3076
  26.5 0.7 %copy-start.2 = (f32[1,128]{1,0:T(1,128)S(1)}, f32[1,128]{1,0:T(1,128)}, u32[]{:S(2)}) copy-start(f32[1,128]{1,0:T(1,128)} %get-tuple-element.9) | copy-start | bytes 1540
  27.7 1.3 %copy-start = (bf16[32,256]{1,0:T(8,128)(2,1)S(1)}, bf16[32,256]{1,0:T(8,128)(2,1)}, u32[]{:S(2)}) copy-start(bf16[32,256]{1,0:T(8,128)(2,1)} %get-tuple-element.19) | copy-start | bytes 49156

commit v2 on v1

--- a/solution.py
+++ b/solution.py
@@ -32,10 +32,10 @@
     rows_n, cols_n,
     src_ref, tgt_ref, lsrc_ref, ltgt_ref, tpot_ref,
     spot_ref, npot_ref, smap_ref, tmap_ref,
-    tgts, srcs, logs, cost, base, lse_cols, pair, pairs, part, parts,
-    z_send, z_recv, y_send, y_recv, x_send, x_recv, c_send, c_recv,
+    lsrc, tgts, srcs, logs, cost, base, lse_cols, pair, pairs, part, parts,
+    z_send, z_recv, y_send, y_recv, x_send, x_recv, d_send, d_recv, c_send, c_recv,
     zs_send, zs_recv, ys_send, ys_recv, v_send, v_recv,
-    m_send, m_recv, p_send, p_recv,
+    m_send, m_recv, p_send, p_recv, in_sem,
 ):
     row, col = lax.axis_index("row"), lax.axis_index("col")
     half_c, half_r = cols_n // 2, rows_n // 2
@@ -55,30 +55,43 @@
             device_id=(to_row, to_col), device_id_type=MESH,
         )
 
-    barrier = pltpu.get_barrier_semaphore()
-    for step in range(1, cols_n):
-        pl.semaphore_signal(barrier, inc=1, device_id=(row, lax.rem(col + step, cols_n)), device_id_type=MESH)
-    for step in range(1, rows_n):
-        pl.semaphore_signal(barrier, inc=1, device_id=(lax.rem(row + step, rows_n), col), device_id_type=MESH)
-
-    tgts[zi, yi, xi, ci] = tgt_ref[...]
-    srcs[zi, yi] = src_ref[...]
     here = pl.ds(pl.multiple_of(col * mine, mine), mine)
-    logs[0:1, here] = ltgt_ref[...]
-    logs[1:2, here] = tpot_ref[...]
-    pl.semaphore_wait(barrier, cols_n - 1 + rows_n - 1)
-
+    loads = (
+        pltpu.make_async_copy(tgt_ref, tgts.at[zi, yi, xi, ci], in_sem.at[0]),
+        pltpu.make_async_copy(src_ref, srcs.at[zi, yi], in_sem.at[1]),
+        pltpu.make_async_copy(ltgt_ref, logs.at[0:1, here], in_sem.at[2]),
+        pltpu.make_async_copy(tpot_ref, logs.at[1:2, here], in_sem.at[3]),
+        pltpu.make_async_copy(lsrc_ref, lsrc, in_sem.at[4]),
+    )
     other_y, other_c = 1 - yi, 1 - ci
     y_col = zi * 2 + other_y
     c_row = xi * 2 + other_c
 
+    barrier = pltpu.get_barrier_semaphore()
+
+    def greet(to_row, to_col):
+        pl.semaphore_signal(barrier, inc=1, device_id=(to_row, to_col), device_id_type=MESH)
+
+    for step in range(1, cols_n):
+        greet(row, lax.rem(col + step, cols_n))
+    for step in range(1, rows_n):
+        greet(lax.rem(row + step, rows_n), col)
+    for step in range(1, half_r):
+        greet(lax.rem(xi + step, half_r) * 2 + ci, y_col)
+    for load in loads:
+        load.start()
+    pl.semaphore_wait(barrier, cols_n - 1 + rows_n - 1 + half_r - 1)
+    loads[0].wait()
+
     def z_copy(step):
         dst = lax.rem(zi + step, half_c)
-        return copy(tgt_ref, tgts.at[zi, yi, xi, ci], z_send.at[step], z_recv.at[step], row, dst * 2 + yi)
+        block = tgts.at[zi, yi, xi, ci]
+        return copy(block, block, z_send.at[step], z_recv.at[step], row, dst * 2 + yi)
 
     def zs_copy(step):
         dst = lax.rem(zi + step, half_c)
-        return copy(src_ref, srcs.at[zi, yi], zs_send.at[step], zs_recv.at[step], row, dst * 2 + yi)
+        block = srcs.at[zi, yi]
+        return copy(block, block, zs_send.at[step], zs_recv.at[step], row, dst * 2 + yi)
 
     def y_copy(step):
         which = lax.rem(zi - step + half_c, half_c)
@@ -90,10 +103,15 @@
         block = srcs.at[which, yi]
         return copy(block, block, ys_send.at[step], ys_recv.at[step], row, y_col)
 
-    def x_copy(step, group):
-        block = tgts.at[:, lax.rem(yi + group, 2), xi, ci]
+    def x_copy(step, lag):
+        block = tgts.at[lax.rem(zi - lag + half_c, half_c), yi, xi, ci]
         to_row = lax.rem(xi + step, half_r) * 2 + ci
-        return copy(block, block, x_send.at[step, group], x_recv.at[step, group], to_row, col)
+        return copy(block, block, x_send.at[step, lag], x_recv.at[step, lag], to_row, col)
+
+    def d_copy(step, lag):
+        block = tgts.at[lax.rem(zi - lag + half_c, half_c), yi, xi, ci]
+        to_row = lax.rem(xi + step, half_r) * 2 + ci
+        return copy(block, block, d_send.at[step, lag], d_recv.at[step, lag], to_row, y_col)
 
     def c_copy(step, group):
         which = lax.rem(xi - step + half_r, half_r)
@@ -103,34 +121,42 @@
     def v_copy(step):
         return copy(logs.at[:, here], logs.at[:, here], v_send.at[step], v_recv.at[step], row, lax.rem(col + step, cols_n))
 
-    y_first = y_copy(0)
-    y_first.start()
+    def plane(lag):
+        for step in range(1, half_r):
+            d_copy(step, lag).start()
+            x_copy(step, lag).start()
+        y_copy(lag).start()
+
     for step in range(1, half_c):
         z_copy(step).start()
+    plane(0)
+    loads[1].wait()
+    for step in range(1, half_c):
+        zs_copy(step).start()
     ys_copy(0).start()
-    for step in range(1, half_c):
-        zs_copy(step).start()
+    for load in loads[2:]:
+        load.wait()
     for step in range(1, cols_n):
         v_copy(step).start()
 
     for step in range(1, half_c):
         z_copy(step).wait_recv()
-        y_copy(step).start()
-    for step in range(1, half_r):
-        x_copy(step, 0).start()
+        plane(step)
     c_copy(0, 0).start()
     for step in range(1, half_c):
         zs_copy(step).wait_recv()
         ys_copy(step).start()
     for step in range(half_c):
         y_copy(step).wait_recv()
+    c_copy(0, 1).start()
     for step in range(1, half_r):
-        x_copy(step, 1).start()
-    c_copy(0, 1).start()
-    for group in range(2):
-        for step in range(1, half_r):
-            x_copy(step, group).wait_recv()
-            c_copy(step, group).start()
+        for lag in range(half_c):
+            x_copy(step, lag).wait_recv()
+        c_copy(step, 0).start()
+    for step in range(1, half_r):
+        for lag in range(half_c):
+            d_copy(step, lag).wait_recv()
+        c_copy(step, 1).start()
     for step in range(half_c):
         ys_copy(step).wait_recv()
     for step in range(1, cols_n):
@@ -179,7 +205,7 @@
 
     repeat(rows // own, first_pass)
     spot_ref[...] = jnp.transpose(base[...])[0:1, :] * (-epsilon * LN2)
-    source_logs = jnp.transpose(jnp.broadcast_to(lsrc_ref[...], (base.shape[1], rows)))
+    source_logs = jnp.transpose(jnp.broadcast_to(lsrc[...], (base.shape[1], rows)))
     base[...] = source_logs * LOG2E - base[...]
 
     def column_pass(index):
@@ -249,16 +275,23 @@
     for step in range(half_c):
         y_copy(step).wait_send()
         ys_copy(step).wait_send()
+        for jump in range(1, half_r):
+            x_copy(jump, step).wait_send()
+            d_copy(jump, step).wait_send()
     for group in range(2):
         for step in range(half_r):
-            if step:
-                x_copy(step, group).wait_send()
             c_copy(step, group).wait_send()
     for step in range(1, cols_n):
         v_copy(step).wait_send()
     for step in range(1, rows_n):
         m_copy(step).wait_send()
         p_copy(step).wait_send()
+
+
+def write_out(*refs):
+    half = len(refs) // 2
+    for src, dst in zip(refs[:half], refs[half:]):
+        dst[...] = src[...]
 
 
 def solution(mesh):
@@ -272,17 +305,20 @@
         f32, bf16 = jnp.float32, jnp.bfloat16
         dma = pltpu.SemaphoreType.DMA
         vmem = pl.BlockSpec(memory_space=pltpu.VMEM)
-        spot, npot, smap, tmap = pl.pallas_call(
+        shapes = (
+            jax.ShapeDtypeStruct((1, rows), f32),
+            jax.ShapeDtypeStruct((1, mine), f32),
+            jax.ShapeDtypeStruct((own, width), bf16),
+            jax.ShapeDtypeStruct((own, width), bf16),
+        )
+        held = 2 * rows * targets + 2 * targets * width
+        results = pl.pallas_call(
             functools.partial(kernel, rows_n, cols_n),
-            out_shape=(
-                jax.ShapeDtypeStruct((1, rows), f32),
-                jax.ShapeDtypeStruct((1, mine), f32),
-                jax.ShapeDtypeStruct((own, width), bf16),
-                jax.ShapeDtypeStruct((own, width), bf16),
-            ),
-            in_specs=[vmem] * 5,
+            out_shape=shapes,
+            in_specs=[pl.BlockSpec(memory_space=pltpu.HBM)] * 5,
             out_specs=(vmem,) * 4,
             scratch_shapes=[
+                pltpu.VMEM((1, rows), f32),
                 pltpu.VMEM((half_c, 2, half_r, 2, own, width), bf16),
                 pltpu.VMEM((half_c, 2, own, width), bf16),
                 pltpu.VMEM((2, targets), f32),
@@ -295,18 +331,23 @@
                 pltpu.VMEM((rows_n - 1, own, width), f32),
                 dma((half_c,)), dma((half_c,)),
                 dma((half_c,)), dma((half_c,)),
-                dma((half_r, 2)), dma((half_r, 2)),
+                dma((half_r, half_c)), dma((half_r, half_c)),
+                dma((half_r, half_c)), dma((half_r, half_c)),
                 dma((half_r, 2)), dma((half_r, 2)),
                 dma((half_c,)), dma((half_c,)),
                 dma((half_c,)), dma((half_c,)),
                 dma((cols_n,)), dma((cols_n,)),
                 dma((rows_n,)), dma((rows_n,)),
                 dma((rows_n,)), dma((rows_n,)),
+                dma((5,)),
             ],
             compiler_params=pltpu.CompilerParams(
-                collective_id=0, has_side_effects=True, vmem_limit_bytes=56 * 1024 * 1024
+                collective_id=0, has_side_effects=True, vmem_limit_bytes=min(56, 14 + 2 * held // 2**20) * 2**20
             ),
         )(src_points, tgt_points, log_src[None, :], log_tgt[None, :], tgt_potential[None, :])
+        spot, npot, smap, tmap = pl.pallas_call(
+            write_out, out_shape=shapes, in_specs=[vmem] * 4, out_specs=(vmem,) * 4
+        )(*results)
         return spot[0], npot[0], smap, tmap
 
     in_specs = (P(("row", "col"), None), P(("col", "row"), None), P("row"), P("col"), P("col"))

time: 29.9 us -> 28.2 us (0.943)
  Pallas kernels: 25.2 us -> 23.3 us
    pallas_call x1 -> x2, Pallas kernels: 25.2 us -> 23.3 us  [the longest x1 22 us: body(): pl.pallas_call(functools.partial(kernel, rows_n, cols_n), out_shape=shape...]
    unnamed x10 -> x18, local copies, waits for them, and re-layouts: 3.79 us -> 3.84 us
where the time goes in v2:
time: 28.2 us; the launch traced here: 27.9 us
  Pallas kernels  23.3 us (83%)
  local copies, waits for them, and re-layouts  3.84 us (14%)
  between operations  0.68 us (2%)
    pallas_call x1, Pallas kernels, body(): pl.pallas_call(functools.partial(kernel, rows_n, cols_n), out_shape=shape...  22 us
    unnamed x18, local copies, waits for them, and re-layouts  3.84 us
    pallas_call x1, Pallas kernels, body(): pl.pallas_call(write_out, out_shape=shapes, in_specs=[vmem] * 4, out_spec...  1.36 us

profile of v2, /device:TPU:0, one launch (start us, length us, event | category | flops | bytes accessed | tf_op | source)
XLA Modules:
  0.0 27.9 jit_solution(6313609254335647135)
XLA Ops:
  0.6 0.0 copy-start.7
  0.6 0.0 copy-start.4
  0.7 0.0 copy-start.6
  0.7 0.6 %copy-done.7 = f32[128]{0:T(128)S(1)} copy-done((f32[128]{0:T(128)S(1)}, f32[128]{0:T(128)}, u32[]{:S(2)}) %copy-start.7) | copy-done | bytes 536
  1.3 0.0 copy-done.4
  1.3 0.0 copy-done.6
  1.3 0.0 copy-start
  1.3 0.7 %copy-done = bf16[32,256]{1,0:T(8,128)(2,1)S(1)} copy-done((bf16[32,256]{1,0:T(8,128)(2,1)S(1)}, bf16[32,256]{1,0:T(8,128)(2,1)}, u32[]{:S(2)}) %copy-start) | copy-done | bytes 16408
  2.0 0.0 copy-start.1
  2.1 0.7 %copy-done.1 = bf16[32,256]{1,0:T(8,128)(2,1)S(1)} copy-done((bf16[32,256]{1,0:T(8,128)(2,1)S(1)}, bf16[32,256]{1,0:T(8,128)(2,1)}, u32[]{:S(2)}) %copy-start.1) | copy-done | bytes 16408
  2.8 22.0 %shard_map.84 = (f32[1,256]{1,0:T(1,128)S(1)}, f32[1,128]{1,0:T(1,128)S(1)}, bf16[32,256]{1,0:T(8,128)(2,1)S(1)}, bf16[32,256]{1,0:T(8,128)(2,1)S(1)}) custom-call(bf16[32,256]{1,0:T(8,128)(2,1)S(1)} %copy-done, bf16[32,256]{1,0:T(8,128)(2,1)S(1)} %copy-done.1, f32[1,256]{1,0:T(1,128)S(1)} %bitcast.5, f32[1,128]{1,0:T(1,128)S(1)} %bitcast.6, ...), custom_call_target="tpu_custom_call" | custom-call | tf_op jit(solution)/shard_map/pallas_call | solution.py:315
  24.7 0.0 copy-start.2
  24.8 0.6 %copy-done.2 = bf16[32,256]{1,0:T(8,128)(2,1)} copy-done((bf16[32,256]{1,0:T(8,128)(2,1)}, bf16[32,256]{1,0:T(8,128)(2,1)S(1)}, u32[]{:S(2)}) %copy-start.2) | copy-done | bytes 16408
  25.4 0.0 copy-start.3
  25.4 0.6 %copy-done.3 = bf16[32,256]{1,0:T(8,128)(2,1)} copy-done((bf16[32,256]{1,0:T(8,128)(2,1)}, bf16[32,256]{1,0:T(8,128)(2,1)S(1)}, u32[]{:S(2)}) %copy-start.3) | copy-done | bytes 16408
  26.0 0.0 copy-start.8
  26.0 0.0 copy-start.5
  26.0 0.5 %copy-done.8 = f32[1,128]{1,0:T(1,128)} copy-done((f32[1,128]{1,0:T(1,128)}, f32[1,128]{1,0:T(1,128)S(1)}, u32[]{:S(2)}) %copy-start.8) | copy-done | bytes 536
  26.5 0.0 copy-done.5
  26.5 1.4 %shard_map.85 = (f32[1,256]{1,0:T(1,128)}, f32[1,128]{1,0:T(1,128)}, bf16[32,256]{1,0:T(8,128)(2,1)}, bf16[32,256]{1,0:T(8,128)(2,1)}) custom-call(f32[1,256]{1,0:T(1,128)} %copy-done.5, f32[1,128]{1,0:T(1,128)} %copy-done.8, bf16[32,256]{1,0:T(8,128)(2,1)} %copy-done.2, bf16[32,256]{1,0:T(8,128)(2,1)} %copy-done.3), custom_call_target="tpu_custom_call" | custom-call | tf_op jit(solution)/shard_map/pallas_call | solution.py:348
Async XLA Ops:
  0.6 0.7 %copy-start.7 = (f32[128]{0:T(128)S(1)}, f32[128]{0:T(128)}, u32[]{:S(2)}) copy-start(f32[128]{0:T(128)} %param.9) | copy-start | bytes 1540
  0.6 0.7 %copy-start.4 = (f32[256]{0:T(256)S(1)}, f32[256]{0:T(256)}, u32[]{:S(2)}) copy-start(f32[256]{0:T(256)} %param.7) | copy-start | bytes 3076
  0.7 0.7 %copy-start.6 = (f32[128]{0:T(128)S(1)}, f32[128]{0:T(128)}, u32[]{:S(2)}) copy-start(f32[128]{0:T(128)} %param.8) | copy-start | bytes 1540
  1.3 0.7 %copy-start = (bf16[32,256]{1,0:T(8,128)(2,1)S(1)}, bf16[32,256]{1,0:T(8,128)(2,1)}, u32[]{:S(2)}) copy-start(bf16[32,256]{1,0:T(8,128)(2,1)} %src_ref.1) | copy-start | bytes 49156
  2.0 0.7 %copy-start.1 = (bf16[32,256]{1,0:T(8,128)(2,1)S(1)}, bf16[32,256]{1,0:T(8,128)(2,1)}, u32[]{:S(2)}) copy-start(bf16[32,256]{1,0:T(8,128)(2,1)} %tgt_ref.1) | copy-start | bytes 49156
  24.7 0.6 %copy-start.2 = (bf16[32,256]{1,0:T(8,128)(2,1)}, bf16[32,256]{1,0:T(8,128)(2,1)S(1)}, u32[]{:S(2)}) copy-start(bf16[32,256]{1,0:T(8,128)(2,1)S(1)} %get-tuple-element.14.refs_2_) | copy-start | bytes 49156
  25.4 0.6 %copy-start.3 = (bf16[32,256]{1,0:T(8,128)(2,1)}, bf16[32,256]{1,0:T(8,128)(2,1)S(1)}, u32[]{:S(2)}) copy-start(bf16[32,256]{1,0:T(8,128)(2,1)S(1)} %get-tuple-element.15.refs_3_) | copy-start | bytes 49156
  26.0 0.5 %copy-start.8 = (f32[1,128]{1,0:T(1,128)}, f32[1,128]{1,0:T(1,128)S(1)}, u32[]{:S(2)}) copy-start(f32[1,128]{1,0:T(1,128)S(1)} %get-tuple-element.13.refs_1_) | copy-start | bytes 1540
  26.0 0.5 %copy-start.5 = (f32[1,256]{1,0:T(1,128)}, f32[1,256]{1,0:T(1,128)S(1)}, u32[]{:S(2)}) copy-start(f32[1,256]{1,0:T(1,128)S(1)} %get-tuple-element.12.refs_0_) | copy-start | bytes 3076
